TPU v7x, 32 devices: a whole 2x2x4 slice. The times are simulated.
32 devices in a mesh: tile: 8 (over y, x, core), node: 4 (over z).
Axes of the slice: x: 2, y: 2, z: 4, core: 2. Of those that a mesh axis runs over, the one named last changes fastest.
Arguments:
- mask_field: float32 [512, 1024], P(None, 'tile'), may hold values from -1 to 1
- kernel_taps: float32 [4, 8, 2, 48, 65], P('node'), may hold values from -0.5 to 0.5
- kernel_weights: float32 [4, 8], P('node'), may hold values from 0.02 to 0.2
- node_weights: float32 [4], replicated, may hold values from 0.125 to 0.5
- node_index: int32 [4, 2], replicated, may hold values from 0 to 4
- freq_index: int32 [48], replicated, may hold values from -256 to 255, as said below
- chaos_weights: float32 [15], replicated, may hold values from 1 to 4
- target: bfloat16 [15, 512, 1024], P(None, None, 'tile'), may hold values from -3 to 3
Outputs:
- mask_gradient: float32 [512, 1024], P('node', 'tile')
Inputs may be any that keep to these rules, and one draw needn't show every extreme that they name: `freq_index`: 48 distinct frequencies.
All inputs are finite; a program needn't handle non-finite values.
Results may differ from a plain program's by a relative error of at most 0.00085.
Values may be sent and summed in bfloat16 or wider, within the bound.
A program may use at most 64 MiB of HBM per device.

v0:
```python
import functools
import math

import jax
import jax.numpy as jnp
import ml_dtypes
import numpy as np
from jax import lax
from jax.experimental import pallas as pl
from jax.experimental.pallas import tpu as pltpu
from jax.sharding import PartitionSpec as P

LEVELS = 5
DEGREES = 5
MESH = pl.DeviceIdType.MESH
bf16 = jnp.bfloat16
f32 = jnp.float32
resist_slope = 4.0
resist_level = 0.6


def split(value):
    high = value.astype(bf16)
    return high, (value - high.astype(f32)).astype(bf16)


def mm(left, right):
    return jnp.dot(left, right, preferred_element_type=f32)


def mm3(left, right):
    count = left[0].shape[0]
    both = mm(jnp.concatenate(left, 0), right[0])
    return both[:count] + (mm(left[0], right[1]) + both[count:])


def half_turn_cosine(step, half):
    folded = jnp.abs((step & (2 * half - 1)) - half).astype(f32)
    t = folded * (2.0 / half) - 1.0
    s = t * t
    acc = jnp.full_like(t, 5.6921729e-8)
    for c in (-3.5988432e-6, 1.6044118e-4, -4.6817541e-3, 7.9692626e-2, -0.64596410, 1.57079633):
        acc = acc * s + c
    return acc * t


def encode(value):
    scaled = value * 2.0**20
    square = scaled * scaled
    fourth = square * square
    return jnp.where(value < 0.0, -fourth, fourth).astype(bf16)


def decode(code):
    code = code.astype(f32)
    size = jnp.sqrt(jnp.sqrt(jnp.abs(code))) * 2.0**-20
    return jnp.where(code < 0.0, -size, size)


def legendre(u):
    s = u * u
    return [None, u, 1.5 * s - 0.5, (2.5 * s - 1.5) * u, (4.375 * s - 3.75) * s + 0.375]


def level(index):
    return index.astype(f32) * (2.0 / (LEVELS - 1)) - 1.0


def basis_of(node_index, node):
    focus = legendre(level(node_index[0, node]))
    dose = legendre(level(node_index[1, node]))
    terms = []
    for degree in range(DEGREES):
        for p in range(degree, -1, -1):
            a, b = focus[p], dose[degree - p]
            terms.append(1.0 if a is None and b is None else b if a is None else a if b is None else a * b)
    return terms


def column_tables(cols, radius, freq_count):
    ring = 2 * cols
    w = np.arange(ring)
    angle = 2 * np.pi * ((w[:, None] * w[None, :]) % ring) / ring
    direct = np.concatenate([np.cos(angle), np.sin(angle)], 1)
    out = 2 * np.pi * ((w[:, None] * (np.arange(cols) + cols - radius)[None, :]) % ring) / ring
    c, s = np.cos(out), np.sin(out)
    back = np.concatenate([np.concatenate([c, s], 1), np.concatenate([-s, c], 1)], 0)
    back = back / (ring * math.sqrt(freq_count))
    pieces = []
    for table in (direct, back, back.T):
        high = table.astype(ml_dtypes.bfloat16)
        low = (table - high.astype(np.float64)).astype(ml_dtypes.bfloat16)
        pieces.append(np.stack([high, low]))
    return pieces


def kernel(
    tiles, nodes, radius,
    mask_hbm, taps_hbm, kernel_weights_hbm, node_weights_hbm, node_index_hbm, freq_hbm, chaos_weights_hbm, target,
    direct_hbm, back_hbm, back_t_hbm,
    out,
    kernel_weights, node_weights, node_index, freq, chaos_weights,
    mask, taps, direct, back, back_t,
    freq_rows, freq_lanes, cos_in, sin_in, trans, own_table, padded_taps, gains,
    own_spec, halo, stacked, cos_part, sin_part, resist, own_image, images, term,
    push, pressure, own_pressure, given, dfield, dparts, dedges, zin, ein, total, gathered,
    local_sem, halo_send, halo_recv, image_send, image_recv, push_send, push_recv,
    z_send, z_recv, e_send, e_recv, g_send, g_recv,
):
    tile, node = lax.axis_index("tile"), lax.axis_index("node")
    right, left = lax.rem(tile + 1, tiles), lax.rem(tile + tiles - 1, tiles)
    rows, cols = mask.shape
    half = rows // 2
    chunk = half // nodes
    freq_count = freq.shape[0]
    terms = chaos_weights.shape[0]
    kernels = taps.shape[0] // 2
    share = 2 * freq_count // nodes

    def after(d):
        return lax.rem(node + d, nodes)

    def before(d):
        return lax.rem(node + nodes - d, nodes)

    barrier = pltpu.get_barrier_semaphore()
    for d in range(1, nodes):
        pl.semaphore_signal(barrier, inc=1, device_id=(tile, after(d)), device_id_type=MESH)
    for d in range(nodes):
        pl.semaphore_signal(barrier, inc=1, device_id=(right, after(d)), device_id_type=MESH)
        pl.semaphore_signal(barrier, inc=1, device_id=(left, after(d)), device_id_type=MESH)

    loads = []
    for i, (source, held) in enumerate((
        (mask_hbm, mask), (direct_hbm, direct), (taps_hbm, taps), (back_hbm, back), (back_t_hbm, back_t),
        (kernel_weights_hbm, kernel_weights), (node_weights_hbm, node_weights),
        (node_index_hbm, node_index), (freq_hbm, freq), (chaos_weights_hbm, chaos_weights),
    )):
        loads.append(pltpu.make_async_copy(source, held, local_sem.at[i + 2]))
    for load in [loads[8]] + loads[:3] + loads[5:8] + loads[9:]:
        load.start()
    upper = pltpu.make_async_copy(
        target.at[:, pl.ds(pl.multiple_of(node * chunk, chunk), chunk), :], term.at[0], local_sem.at[0]
    )
    lower = pltpu.make_async_copy(
        target.at[:, pl.ds(pl.multiple_of(rows - (node + 1) * chunk, chunk), chunk), :],
        term.at[1], local_sem.at[1],
    )
    upper.start()
    lower.start()
    for load in loads[3:5]:
        load.start()

    loads[8].wait()
    row_id = lax.broadcasted_iota(jnp.int32, freq_rows.shape, 0)
    lane_id = lax.broadcasted_iota(jnp.int32, freq_lanes.shape, 1) % freq_count
    by_row = jnp.zeros(freq_rows.shape, jnp.int32)
    by_lane = jnp.zeros(freq_lanes.shape, jnp.int32)
    for i in range(freq_count):
        by_row = jnp.where(row_id == i, freq[i], by_row)
        by_lane = jnp.where(lane_id == i, freq[i], by_lane)
    freq_rows[...] = by_row
    freq_lanes[...] = by_lane

    place = lax.broadcasted_iota(jnp.int32, (freq_count, half), 1)
    step = freq_rows[:, :1] * (2 * place + 1)
    c_high, c_low = split(half_turn_cosine(step, rows))
    s_high, s_low = split(half_turn_cosine(step - half, rows))
    trans[0, :, :half] = c_high
    trans[1, :, :half] = c_low
    trans[0, :, half:] = s_high
    trans[1, :, half:] = s_low

    ri = lax.broadcasted_iota(jnp.int32, (half, half), 0)
    ci = lax.broadcasted_iota(jnp.int32, (half, half), 1)
    mirror = jnp.where(ri + ci == half - 1, 1.0, 0.0).astype(bf16)
    loads[0].wait()
    m_high, m_low = split(mask[half:, :])
    mirrored = mm(mirror, m_high) + mm(mirror, m_low)
    top = mask[:half, :]
    norm = 1.0 / math.sqrt(rows)
    own_spec[:freq_count, :] = mm3((c_high, c_low), split(top + mirrored)) * norm
    own_spec[freq_count:, :] = mm3((s_high, s_low), split(top - mirrored)) * -norm

    pl.semaphore_wait(barrier, 3 * nodes - 1)
    halo_copies = []
    for side, to in ((0, right), (1, left)):
        halo_copies.append(pltpu.make_async_remote_copy(
            src_ref=own_spec, dst_ref=halo.at[side], send_sem=halo_send.at[side],
            recv_sem=halo_recv.at[side], device_id=(to, node), device_id_type=MESH,
        ))
        halo_copies[-1].start()

    wide = 3 * freq_count
    place = lax.broadcasted_iota(jnp.int32, (half, wide), 0)
    lane = lax.broadcasted_iota(jnp.int32, (half, wide), 1)
    middle = (lane >= freq_count) & (lane < 2 * freq_count)
    step = freq_lanes[:1, :wide] * (2 * place + 1)
    for table, value in ((cos_in, half_turn_cosine(step, rows)), (sin_in, half_turn_cosine(step - half, rows))):
        rounded = value.astype(bf16).astype(f32)
        table[...] = jnp.where(middle, value - rounded, rounded).astype(bf16)

    own_rows = rows // nodes
    place = lax.broadcasted_iota(jnp.int32, (own_rows, 2 * freq_count), 0) + node * own_rows
    lane = lax.broadcasted_iota(jnp.int32, (own_rows, 2 * freq_count), 1)
    step = freq_lanes[:1, : 2 * freq_count] * (2 * place + 1)
    step = jnp.where(lane < freq_count, step, step + half)
    own_table[0], own_table[1] = split(half_turn_cosine(step, rows) * norm)

    padded_taps[...] = jnp.zeros(padded_taps.shape, f32)
    loads[1].wait()
    loads[2].wait()
    for i in range(2 * kernels):
        padded_taps[i * freq_count : (i + 1) * freq_count, : 2 * radius + 1] = taps[i]
    near = padded_taps.shape[1]
    t = mm3(split(padded_taps[...]), (direct[0, :near, :], direct[1, :near, :]))
    ring = 2 * cols
    for k in range(kernels):
        re = t[2 * k * freq_count : (2 * k + 1) * freq_count]
        im = t[(2 * k + 1) * freq_count : (2 * k + 2) * freq_count]
        gains[k, :, :ring] = re[:, :ring] - im[:, ring:]
        gains[k, :, ring:] = re[:, ring:] + im[:, :ring]

    ri = lax.broadcasted_iota(jnp.int32, (chunk, chunk), 0)
    ci = lax.broadcasted_iota(jnp.int32, (chunk, chunk), 1)
    small_mirror = jnp.where(ri + ci == chunk - 1, 1.0, 0.0).astype(bf16)
    upper.wait()
    lower.wait()
    turned = mm(small_mirror, jnp.concatenate([term[1, j] for j in range(terms)], 1)).astype(bf16)
    for j in range(terms):
        term[1, j] = turned[:, j * cols : (j + 1) * cols]

    for copy in halo_copies:
        copy.wait()
    lane = lax.broadcasted_iota(jnp.int32, (2 * freq_count, cols), 1)
    keep_left = jnp.where((lane >= cols - radius) & (tile > 0), 1.0, 0.0)
    keep_right = jnp.where((lane < radius) & (tile < tiles - 1), 1.0, 0.0)
    around = jnp.concatenate([halo[0] * keep_left + halo[1] * keep_right, own_spec[...]], 1)
    t = mm3(split(around), (direct[0], direct[1]))
    a_re = t[:freq_count, :ring] + t[freq_count:, ring:]
    a_im = t[freq_count:, :ring] - t[:freq_count, ring:]
    products = []
    for k in range(kernels):
        g_re, g_im = gains[k, :, :ring], gains[k, :, ring:]
        products.append(jnp.concatenate([a_re * g_re - a_im * g_im, a_re * g_im + a_im * g_re], 1))
    loads[3].wait()
    band = mm3(split(jnp.concatenate(products, 0)), (back[0], back[1]))
    for k in range(kernels):
        high, low = split(band[k * freq_count : (k + 1) * freq_count])
        for part in range(2):
            at = (part * kernels + k) * cols
            source = slice(part * cols, (part + 1) * cols)
            stacked[:freq_count, at : at + cols] = high[:, source]
            stacked[freq_count : 2 * freq_count, at : at + cols] = high[:, source]
            stacked[2 * freq_count :, at : at + cols] = low[:, source]

    def image_copy(d, part):
        return pltpu.make_async_remote_copy(
            src_ref=own_image.at[after(d), part], dst_ref=images.at[d, part], send_sem=image_send.at[d, part],
            recv_sem=image_recv.at[d, part], device_id=(tile, after(d)), device_id_type=MESH,
        )

    for load in loads[5:8] + loads[9:]:
        load.wait()
    dose = 1.0 + 0.1 * level(node_index[1, node])
    side = kernels * cols
    cos_part[...] = mm(cos_in[...], stacked[...])
    sin_part[...] = mm(sin_in[...], stacked[...])

    def fields(row, count, k):
        p = cos_part[pl.ds(row, count), k * cols : (k + 1) * cols]
        t = cos_part[pl.ds(row, count), side + k * cols : side + (k + 1) * cols]
        r = sin_part[pl.ds(row, count), k * cols : (k + 1) * cols]
        q = sin_part[pl.ds(row, count), side + k * cols : side + (k + 1) * cols]
        return p - q, r + t, p + q, t - r

    piece = images.shape[3]
    parts = chunk // piece

    @pl.loop(0, parts)
    def _(part):
        @pl.loop(0, nodes)
        def _(i):
            d = lax.rem(i + 1, nodes)
            mine = after(d)
            at = pl.multiple_of(mine * chunk + part * piece, piece)
            first = jnp.zeros((piece, cols), f32)
            second = jnp.zeros((piece, cols), f32)
            for k in range(kernels):
                a, b, c, e = fields(at, piece, k)
                weight = kernel_weights[0, k]
                first = first + weight * (a * a + b * b)
                second = second + weight * (c * c + e * e)
            for h, intensity in ((0, first), (1, second)):
                value = jax.nn.sigmoid(resist_slope * (dose * intensity - resist_level))
                resist[h, pl.ds(at, piece), :] = value
                own_image[mine, part, h] = value.astype(bf16)

            @pl.when(d != 0)
            def _():
                image_copy(d, part).start()

    images[0] = own_image[node]

    sources = [before(d) for d in range(nodes)]
    bases = [basis_of(node_index, n) for n in sources]
    weights = [node_weights[n] for n in sources]
    scaled = [[weights[d] * b for b in bases[d]] for d in range(nodes)]

    def push_copy(d, part):
        return pltpu.make_async_remote_copy(
            src_ref=push.at[d, part], dst_ref=pressure.at[d, part], send_sem=push_send.at[d, part],
            recv_sem=push_recv.at[d, part], device_id=(tile, before(d)), device_id_type=MESH,
        )

    @pl.loop(0, parts)
    def _(part):
        for d in range(1, nodes):
            image_copy(d, part).wait()

        @pl.loop(0, 2)
        def _(h):
            seen = [images[d, part, h].astype(f32) for d in range(nodes)]
            sums = [None] * nodes
            for j in range(terms):
                coefficient = scaled[0][j] * seen[0]
                for d in range(1, nodes):
                    coefficient = coefficient + scaled[d][j] * seen[d]
                wanted = term[h, j, pl.ds(pl.multiple_of(part * piece, piece), piece), :]
                mixed = chaos_weights[j] * jnp.tanh(coefficient - wanted.astype(f32))
                for d in range(nodes):
                    one = scaled[d][j] * mixed
                    sums[d] = one if sums[d] is None else sums[d] + one
            for d in range(nodes):
                if d:
                    push[d, part, h] = encode(sums[d])
                else:
                    own_pressure[part, h] = sums[d]

        for d in range(1, nodes):
            push_copy(d, part).start()

    @pl.loop(0, parts)
    def _(part):
        @pl.loop(0, nodes)
        def _(d):
            @pl.when(d == 0)
            def _():
                given[...] = own_pressure[part]

            @pl.when(d != 0)
            def _():
                push_copy(d, part).wait()
                given[...] = decode(pressure[d, part])

            at = pl.multiple_of(after(d) * chunk + part * piece, piece)
            slopes = []
            for h in range(2):
                value = resist[h, pl.ds(at, piece), :]
                slopes.append(given[h] * value * (1.0 - value) * (resist_slope * dose))
            for k in range(kernels):
                a, b, c, e = fields(at, piece, k)
                a, b, c, e = a * slopes[0], b * slopes[0], c * slopes[1], e * slopes[1]
                for base, where, value in ((0, 0, a + c), (0, side, b + e), (half, 0, b - e), (half, side, c - a)):
                    high, low = split(value)
                    lanes = slice(where + k * cols, where + (k + 1) * cols)
                    dfield[0, pl.ds(base + at, piece), lanes] = high
                    dfield[1, pl.ds(base + at, piece), lanes] = low

    both = trans[...].reshape(2 * freq_count, 2 * half)
    t = mm(both, dfield[0])
    dband = t[:freq_count] + t[freq_count:] + mm(trans[0], dfield[1])
    pieces = []
    for k in range(kernels):
        one = jnp.concatenate([dband[:, k * cols : (k + 1) * cols], dband[:, side + k * cols : side + (k + 1) * cols]], 1)
        pieces.append(one * (2.0 * kernel_weights[0, k]))
    loads[4].wait()
    t = mm3(split(jnp.concatenate(pieces, 0)), (back_t[0], back_t[1]))
    z_re = jnp.zeros((freq_count, ring), f32)
    z_im = jnp.zeros((freq_count, ring), f32)
    for k in range(kernels):
        d_re = t[k * freq_count : (k + 1) * freq_count, :ring]
        d_im = t[k * freq_count : (k + 1) * freq_count, ring:]
        g_re, g_im = gains[k, :, :ring], gains[k, :, ring:]
        z_re = z_re + (g_re * d_re + g_im * d_im)
        z_im = z_im + (g_re * d_im - g_im * d_re)
    t = mm3(split(jnp.concatenate([z_re, z_im], 0)), (direct[0], direct[1]))
    dspec = jnp.concatenate(
        [t[:freq_count, :ring] - t[freq_count:, ring:], t[:freq_count, ring:] + t[freq_count:, :ring]], 0
    )
    fold = ein.shape[2]
    groups = share // fold
    lane = lax.broadcasted_iota(jnp.int32, (fold, cols), 1)
    for n in range(nodes):
        dparts[n] = dspec[n * share : (n + 1) * share, cols:]
        for side_id in range(2):
            packed = None
            for g in range(groups):
                block = dspec[n * share + g * fold : n * share + (g + 1) * fold, :cols]
                if g == 0:
                    packed = block
                    continue
                moved = pltpu.roll(block, g * radius if side_id == 0 else cols - g * radius, 1)
                there = lane >= g * radius if side_id == 0 else lane < cols - g * radius
                packed = jnp.where(there, moved, packed)
            dedges[side_id, n] = packed

    def z_copy(d):
        return pltpu.make_async_remote_copy(
            src_ref=dparts.at[after(d)], dst_ref=zin.at[d], send_sem=z_send.at[d],
            recv_sem=z_recv.at[d], device_id=(tile, after(d)), device_id_type=MESH,
        )

    def e_copy(d, side_id):
        to = right if side_id == 0 else left
        return pltpu.make_async_remote_copy(
            src_ref=dedges.at[side_id, after(d)], dst_ref=ein.at[side_id, d], send_sem=e_send.at[side_id, d],
            recv_sem=e_recv.at[side_id, d], device_id=(to, after(d)), device_id_type=MESH,
        )

    copies = []
    for d in range(nodes):
        copies += [e_copy(d, 0), e_copy(d, 1)]
        if d:
            copies.append(z_copy(d))
    for copy in copies:
        copy.start()
    for copy in copies:
        copy.wait()
    value = dparts[node]
    from_left, from_right = ein[0, 0], ein[1, 0]
    for d in range(1, nodes):
        value = value + zin[d]
        from_left, from_right = from_left + ein[0, d], from_right + ein[1, d]
    keep_left = jnp.where((lane < radius) & (tile > 0), 1.0, 0.0)
    keep_right = jnp.where((lane >= cols - radius) & (tile < tiles - 1), 1.0, 0.0)
    edges = []
    for g in range(groups):
        a, b = from_left, from_right
        if g:
            a, b = pltpu.roll(a, cols - g * radius, 1), pltpu.roll(b, g * radius, 1)
        edges.append(a * keep_left + b * keep_right)
    value = value + jnp.concatenate(edges, 0)
    total[...] = value
    gathered[node] = value

    def g_copy(d):
        return pltpu.make_async_remote_copy(
            src_ref=total, dst_ref=gathered.at[node], send_sem=g_send.at[d],
            recv_sem=g_recv.at[d], device_id=(tile, after(d)), device_id_type=MESH,
        )

    for d in range(1, nodes):
        g_copy(d).start()
    for d in range(1, nodes):
        g_copy(d).wait()
    summed = jnp.concatenate([gathered[n] for n in range(nodes)], 0)
    out[...] = mm3((own_table[0], own_table[1]), split(summed))


def local(
    tiles, nodes,
    mask_field, kernel_taps, kernel_weights, node_weights, node_index, freq_index, chaos_weights, target,
):
    rows, cols = mask_field.shape
    _, kernels, _, freq_count, tap_count = kernel_taps.shape
    radius = (tap_count - 1) // 2
    half, chunk = rows // 2, rows // 2 // nodes
    terms = chaos_weights.shape[0]
    ring = 2 * cols
    share = 2 * freq_count // nodes
    piece = min(32, chunk)
    fold = 8 if share % 8 == 0 and share // 8 * radius <= cols else share
    direct, back, back_t = column_tables(cols, radius, freq_count)
    vmem = pl.BlockSpec(memory_space=pltpu.VMEM)
    hbm = pl.BlockSpec(memory_space=pl.ANY)
    smem = pltpu.SMEM
    scratch = pltpu.VMEM
    dma = pltpu.SemaphoreType.DMA
    return pl.pallas_call(
        functools.partial(kernel, tiles, nodes, radius),
        out_shape=jax.ShapeDtypeStruct((rows // nodes, cols), f32),
        in_specs=[hbm] * 11,
        out_specs=vmem,
        scratch_shapes=[
            smem(kernel_weights.shape, f32),
            smem(node_weights.shape, f32),
            smem(node_index.shape[::-1], jnp.int32),
            smem(freq_index.shape, jnp.int32),
            smem(chaos_weights.shape, f32),
            scratch((rows, cols), f32),
            scratch((2 * kernels, freq_count, tap_count), f32),
            scratch(direct.shape, bf16),
            scratch(back.shape, bf16),
            scratch(back_t.shape, bf16),
            scratch((freq_count, 128), jnp.int32),
            scratch((8, 256), jnp.int32),
            scratch((half, 3 * freq_count), bf16),
            scratch((half, 3 * freq_count), bf16),
            scratch((2, freq_count, 2 * half), bf16),
            scratch((2, rows // nodes, 2 * freq_count), bf16),
            scratch((2 * kernels * freq_count, 128), f32),
            scratch((kernels, freq_count, 2 * ring), f32),
            scratch((2 * freq_count, cols), f32),
            scratch((2, 2 * freq_count, cols), f32),
            scratch((3 * freq_count, 2 * kernels * cols), bf16),
            scratch((half, 2 * kernels * cols), f32),
            scratch((half, 2 * kernels * cols), f32),
            scratch((2, half, cols), f32),
            scratch((nodes, chunk // piece, 2, piece, cols), bf16),
            scratch((nodes, chunk // piece, 2, piece, cols), bf16),
            scratch((2, terms, chunk, cols), bf16),
            scratch((nodes, chunk // piece, 2, piece, cols), bf16),
            scratch((nodes, chunk // piece, 2, piece, cols), bf16),
            scratch((chunk // piece, 2, piece, cols), f32),
            scratch((2, piece, cols), f32),
            scratch((2, 2 * half, 2 * kernels * cols), bf16),
            scratch((nodes, share, cols), f32),
            scratch((2, nodes, fold, cols), f32),
            scratch((nodes, share, cols), f32),
            scratch((2, nodes, fold, cols), f32),
            scratch((share, cols), f32),
            scratch((nodes, share, cols), f32),
            dma((12,)), dma((2,)), dma((2,)),
            dma((nodes, chunk // piece)), dma((nodes, chunk // piece)), dma((nodes, chunk // piece)), dma((nodes, chunk // piece)),
            dma((nodes,)), dma((nodes,)), dma((2, nodes)), dma((2, nodes)),
            dma((nodes,)), dma((nodes,)),
        ],
        compiler_params=pltpu.CompilerParams(
            collective_id=0, has_side_effects=True, vmem_limit_bytes=63 * 1024 * 1024
        ),
        name="mask_gradient",
    )(
        mask_field, kernel_taps.reshape(2 * kernels, freq_count, tap_count), kernel_weights, node_weights,
        node_index.T, freq_index, chaos_weights, target, direct, back, back_t,
    )


def solution(mesh):
    placed = (
        P(None, "tile"),
        P("node", None, None, None, None),
        P("node", None),
        P(),
        P(),
        P(),
        P(),
        P(None, None, "tile"),
    )
    return jax.shard_map(
        functools.partial(local, mesh.shape["tile"], mesh.shape["node"]),
        mesh=mesh, in_specs=placed, out_specs=P("node", "tile"), check_vma=False,
    )
```

profile of v0, /device:TPU:0, one launch (start us, length us, event | category | flops | bytes accessed | tf_op | source)
XLA Modules:
  0.0 33.4 jit_solution(17316360302441938970)
XLA Ops:
  0.0 31.9 %mask_gradient.1 = f32[128,128]{1,0:T(8,128)} custom-call(f32[512,128]{1,0:T(8,128)} %mask_hbm.1, f32[16,48,65]{2,1,0:T(8,128)} %bitcast.2, f32[1,8]{1,0:T(1,128)} %kernel_weights_hbm.1, f32[4]{0:T(128)} %node_weights_hbm.1, s32[2,4]{1,0:T(2,128)} %bitcast.3, s32[48]{0:T(128)} %freq_hbm.1, f32[15]{0:T(128)} %chaos_weights_hbm.1, ...), custom_call_target="tpu_custom_call" | custom-call | tf_op jit(solution)/shard_map/mask_gradient/pallas_call | solution.py:480
  32.0 1.5 %copy.13 = f32[128,128]{1,0:T(8,128)} copy(f32[128,128]{1,0:T(8,128)} %mask_gradient.1) | data formatting | bytes 131072
where the time goes:
time: 33.6 us; the launch traced here: 33.4 us
  Pallas kernels  31.9 us (95%)
  local copies, waits for them, and re-layouts  1.47 us (4%)
    pallas_call x1, Pallas kernels, local(): pl.pallas_call(functools.partial(kernel, tiles, nodes, radius), out_shape...  31.9 us
    unnamed x1, local copies, waits for them, and re-layouts  1.47 us

commit v1 on v0

--- a/solution.py
+++ b/solution.py
@@ -101,9 +101,9 @@
     out,
     kernel_weights, node_weights, node_index, freq, chaos_weights,
     mask, taps, direct, back, back_t,
-    freq_rows, freq_lanes, cos_in, sin_in, trans, own_table, padded_taps, gains,
-    own_spec, halo, stacked, cos_part, sin_part, resist, own_image, images, term,
-    push, pressure, own_pressure, given, dfield, dparts, dedges, zin, ein, total, gathered,
+    freq_rows, freq_lanes, row_table, scaled, trans, own_table, padded_taps, gains,
+    own_spec, halo, stacked, parts_of, resist, own_image, images, term,
+    push, pressure, own_pressure, given, dfield, dband, dparts, dedges, zin, ein, total, gathered,
     local_sem, halo_send, halo_recv, image_send, image_recv, push_send, push_recv,
     z_send, z_recv, e_send, e_recv, g_send, g_recv,
 ):
@@ -192,13 +192,27 @@
         halo_copies[-1].start()
 
     wide = 3 * freq_count
-    place = lax.broadcasted_iota(jnp.int32, (half, wide), 0)
-    lane = lax.broadcasted_iota(jnp.int32, (half, wide), 1)
+    strip = rows // 8
+    lane = lax.broadcasted_iota(jnp.int32, (strip, wide), 1)
     middle = (lane >= freq_count) & (lane < 2 * freq_count)
-    step = freq_lanes[:1, :wide] * (2 * place + 1)
-    for table, value in ((cos_in, half_turn_cosine(step, rows)), (sin_in, half_turn_cosine(step - half, rows))):
+    strip_row = lax.broadcasted_iota(jnp.int32, (strip, wide), 0)
+
+    @pl.loop(0, 8)
+    def _(i):
+        sine = (i >= 4).astype(jnp.int32)
+        place = strip_row + (i * strip - sine * half)
+        value = half_turn_cosine(freq_lanes[:1, :wide] * (2 * place + 1) - sine * half, rows)
         rounded = value.astype(bf16).astype(f32)
-        table[...] = jnp.where(middle, value - rounded, rounded).astype(bf16)
+        row_table[pl.ds(pl.multiple_of(i * strip, strip), strip), :] = jnp.where(
+            middle, value - rounded, rounded
+        ).astype(bf16)
+
+    for load in loads[5:8] + loads[9:]:
+        load.wait()
+    for d in range(nodes):
+        n = before(d)
+        for j, b in enumerate(basis_of(node_index, n)):
+            scaled[d, j] = node_weights[n] * b
 
     own_rows = rows // nodes
     place = lax.broadcasted_iota(jnp.int32, (own_rows, 2 * freq_count), 0) + node * own_rows
@@ -213,13 +227,19 @@
     for i in range(2 * kernels):
         padded_taps[i * freq_count : (i + 1) * freq_count, : 2 * radius + 1] = taps[i]
     near = padded_taps.shape[1]
-    t = mm3(split(padded_taps[...]), (direct[0, :near, :], direct[1, :near, :]))
     ring = 2 * cols
-    for k in range(kernels):
-        re = t[2 * k * freq_count : (2 * k + 1) * freq_count]
-        im = t[(2 * k + 1) * freq_count : (2 * k + 2) * freq_count]
-        gains[k, :, :ring] = re[:, :ring] - im[:, ring:]
-        gains[k, :, ring:] = re[:, ring:] + im[:, :ring]
+    run = 2 if kernels % 2 == 0 else 1
+
+    @pl.loop(0, kernels // run)
+    def _(i):
+        height = 2 * run * freq_count
+        rows_now = padded_taps[pl.ds(pl.multiple_of(i * height, height), height), :]
+        t = mm3(split(rows_now), (direct[0, :near, :], direct[1, :near, :]))
+        for k in range(run):
+            re = t[2 * k * freq_count : (2 * k + 1) * freq_count]
+            im = t[(2 * k + 1) * freq_count : (2 * k + 2) * freq_count]
+            gains[i * run + k, :, :ring] = re[:, :ring] - im[:, ring:]
+            gains[i * run + k, :, ring:] = re[:, ring:] + im[:, :ring]
 
     ri = lax.broadcasted_iota(jnp.int32, (chunk, chunk), 0)
     ci = lax.broadcasted_iota(jnp.int32, (chunk, chunk), 1)
@@ -260,18 +280,20 @@
             recv_sem=image_recv.at[d, part], device_id=(tile, after(d)), device_id_type=MESH,
         )
 
-    for load in loads[5:8] + loads[9:]:
-        load.wait()
     dose = 1.0 + 0.1 * level(node_index[1, node])
     side = kernels * cols
-    cos_part[...] = mm(cos_in[...], stacked[...])
-    sin_part[...] = mm(sin_in[...], stacked[...])
+    width = 4 * cols if 2 * kernels % 4 == 0 else side
+
+    @pl.loop(0, 2 * side // width)
+    def _(i):
+        lanes = pl.ds(pl.multiple_of(i * width, width), width)
+        parts_of[:, lanes] = mm(row_table[...], stacked[:, lanes])
 
     def fields(row, count, k):
-        p = cos_part[pl.ds(row, count), k * cols : (k + 1) * cols]
-        t = cos_part[pl.ds(row, count), side + k * cols : side + (k + 1) * cols]
-        r = sin_part[pl.ds(row, count), k * cols : (k + 1) * cols]
-        q = sin_part[pl.ds(row, count), side + k * cols : side + (k + 1) * cols]
+        p = parts_of[pl.ds(row, count), k * cols : (k + 1) * cols]
+        t = parts_of[pl.ds(row, count), side + k * cols : side + (k + 1) * cols]
+        r = parts_of[pl.ds(half + row, count), k * cols : (k + 1) * cols]
+        q = parts_of[pl.ds(half + row, count), side + k * cols : side + (k + 1) * cols]
         return p - q, r + t, p + q, t - r
 
     piece = images.shape[3]
@@ -302,11 +324,6 @@
 
     images[0] = own_image[node]
 
-    sources = [before(d) for d in range(nodes)]
-    bases = [basis_of(node_index, n) for n in sources]
-    weights = [node_weights[n] for n in sources]
-    scaled = [[weights[d] * b for b in bases[d]] for d in range(nodes)]
-
     def push_copy(d, part):
         return pltpu.make_async_remote_copy(
             src_ref=push.at[d, part], dst_ref=pressure.at[d, part], send_sem=push_send.at[d, part],
@@ -323,13 +340,13 @@
             seen = [images[d, part, h].astype(f32) for d in range(nodes)]
             sums = [None] * nodes
             for j in range(terms):
-                coefficient = scaled[0][j] * seen[0]
+                coefficient = scaled[0, j] * seen[0]
                 for d in range(1, nodes):
-                    coefficient = coefficient + scaled[d][j] * seen[d]
+                    coefficient = coefficient + scaled[d, j] * seen[d]
                 wanted = term[h, j, pl.ds(pl.multiple_of(part * piece, piece), piece), :]
                 mixed = chaos_weights[j] * jnp.tanh(coefficient - wanted.astype(f32))
                 for d in range(nodes):
-                    one = scaled[d][j] * mixed
+                    one = scaled[d, j] * mixed
                     sums[d] = one if sums[d] is None else sums[d] + one
             for d in range(nodes):
                 if d:
@@ -368,8 +385,13 @@
                     dfield[1, pl.ds(base + at, piece), lanes] = low
 
     both = trans[...].reshape(2 * freq_count, 2 * half)
-    t = mm(both, dfield[0])
-    dband = t[:freq_count] + t[freq_count:] + mm(trans[0], dfield[1])
+
+    @pl.loop(0, 2 * side // width)
+    def _(i):
+        lanes = pl.ds(pl.multiple_of(i * width, width), width)
+        t = mm(both, dfield[0, :, lanes])
+        dband[:, lanes] = t[:freq_count] + t[freq_count:] + mm(trans[0], dfield[1, :, lanes])
+
     pieces = []
     for k in range(kernels):
         one = jnp.concatenate([dband[:, k * cols : (k + 1) * cols], dband[:, side + k * cols : side + (k + 1) * cols]], 1)
@@ -495,8 +517,8 @@
             scratch(back_t.shape, bf16),
             scratch((freq_count, 128), jnp.int32),
             scratch((8, 256), jnp.int32),
-            scratch((half, 3 * freq_count), bf16),
-            scratch((half, 3 * freq_count), bf16),
+            scratch((rows, 3 * freq_count), bf16),
+            smem((nodes, terms), f32),
             scratch((2, freq_count, 2 * half), bf16),
             scratch((2, rows // nodes, 2 * freq_count), bf16),
             scratch((2 * kernels * freq_count, 128), f32),
@@ -504,8 +526,7 @@
             scratch((2 * freq_count, cols), f32),
             scratch((2, 2 * freq_count, cols), f32),
             scratch((3 * freq_count, 2 * kernels * cols), bf16),
-            scratch((half, 2 * kernels * cols), f32),
-            scratch((half, 2 * kernels * cols), f32),
+            scratch((rows, 2 * kernels * cols), f32),
             scratch((2, half, cols), f32),
             scratch((nodes, chunk // piece, 2, piece, cols), bf16),
             scratch((nodes, chunk // piece, 2, piece, cols), bf16),
@@ -515,6 +536,7 @@
             scratch((chunk // piece, 2, piece, cols), f32),
             scratch((2, piece, cols), f32),
             scratch((2, 2 * half, 2 * kernels * cols), bf16),
+            scratch((freq_count, 2 * kernels * cols), f32),
             scratch((nodes, share, cols), f32),
             scratch((2, nodes, fold, cols), f32),
             scratch((nodes, share, cols), f32),

time: 33.6 us -> 34.2 us (1.018)
  Pallas kernels: 31.9 us -> 32.5 us
    pallas_call x1, Pallas kernels: 31.9 us -> 32.5 us  [local(): pl.pallas_call(functools.partial(kernel, tiles, nodes, radius), out_shape...]
where the time goes in v1:
time: 34.2 us; the launch traced here: 34 us
  Pallas kernels  32.5 us (95%)
  local copies, waits for them, and re-layouts  1.47 us (4%)
    pallas_call x1, Pallas kernels, local(): pl.pallas_call(functools.partial(kernel, tiles, nodes, radius), out_shape...  32.5 us
    unnamed x1, local copies, waits for them, and re-layouts  1.47 us

profile of v1, /device:TPU:0, one launch (start us, length us, event | category | flops | bytes accessed | tf_op | source)
XLA Modules:
  0.0 34.0 jit_solution(5480083816382108848)
XLA Ops:
  0.0 32.5 %mask_gradient.1 = f32[128,128]{1,0:T(8,128)} custom-call(f32[512,128]{1,0:T(8,128)} %mask_hbm.1, f32[16,48,65]{2,1,0:T(8,128)} %bitcast.2, f32[1,8]{1,0:T(1,128)} %kernel_weights_hbm.1, f32[4]{0:T(128)} %node_weights_hbm.1, s32[2,4]{1,0:T(2,128)} %bitcast.3, s32[48]{0:T(128)} %freq_hbm.1, f32[15]{0:T(128)} %chaos_weights_hbm.1, ...), custom_call_target="tpu_custom_call" | custom-call | tf_op jit(solution)/shard_map/mask_gradient/pallas_call | solution.py:502
  32.5 1.5 %copy.13 = f32[128,128]{1,0:T(8,128)} copy(f32[128,128]{1,0:T(8,128)} %mask_gradient.1) | data formatting | bytes 131072
